TPU v7x, 128 devices: a whole 4x4x4 slice. The times are simulated.
128 devices in a mesh: ctg: 16 (over y, x), line: 8 (over z, core).
Axes of the slice: x: 4, y: 4, z: 4, core: 2. Of those that a mesh axis runs over, the one named last changes fastest.
Arguments:
- base_flow: float32 [384, 15360], P(None, ('ctg', 'line')), may hold values from -6 to 6
- lodf: bfloat16 [15360, 15360], P('line', 'ctg'), may hold values from -0.3125 to 0.3125
- dual: bfloat16 [15360, 15360], P('line', 'ctg'), may hold values from 0 to 2.5, as said below
- rating: float32 [15360], P('line'), may hold values from 0.3 to 2
- sens: bfloat16 [15360, 2048], P('line', 'ctg'), may hold values from -0.046875 to 0.046875
- fetch_rows: int32 [16, 128, 15], P('ctg'), may hold values from -1 to 119, as said below
- ctg_slot: int32 [15360], P('ctg'), may hold values from 0 to 1919, as said below
Outputs:
- cut: float32 [2048, 384], P(('ctg', 'line'))
Inputs may be any that keep to these rules, and one draw needn't show every extreme that they name: `fetch_rows`: -1 marks an empty slot; other entries are distinct columns of flow holder o's block of 120 lines; some pairs (c, o) may have no live slot, and one flow holder has all 15 slots live for every contingency holder. `ctg_slot`: the 960 contingencies of holder c take distinct slots o * 15 + j, exactly the live entries of fetch_rows[c]. `dual`: zero outside the overloaded pairs, positive on them.
All inputs are finite; a program needn't handle non-finite values.
Results may differ from a plain program's by a relative error of at most 0.0059.
Values may be sent and summed in bfloat16 or wider, within the bound.
A program may use at most 64 MiB of HBM per device.

v0:
```python
import jax
import jax.numpy as jnp
from jax import lax
from jax.sharding import PartitionSpec as P


def soft_excess(flow_sum, rating):
    return jnp.sign(flow_sum) * jnp.maximum(jnp.abs(flow_sum) - rating[None, :], 0.0)


def per_device(base_flow, lodf, dual, rating, sens, fetch_rows, ctg_slot):
    columns_total = base_flow.shape[0]
    requests = fetch_rows[0]
    asked = lax.all_to_all(requests, ("ctg", "line"), split_axis=0, concat_axis=0, tiled=True)
    live_slot = asked >= 0
    columns = jnp.where(live_slot, asked, 0)
    values = jnp.take(base_flow, columns.reshape(-1), axis=1)
    values = values.reshape(columns_total, asked.shape[0], asked.shape[1])
    replies = lax.all_to_all(
        jnp.where(live_slot[None], values, 0.0).astype(jnp.bfloat16),
        ("ctg", "line"),
        split_axis=1,
        concat_axis=1,
        tiled=True,
    )
    slot_flows = replies.reshape(columns_total, -1)
    outage_flow = jnp.take(slot_flows, ctg_slot, axis=1)
    weighted = (dual.astype(jnp.float32) * lodf.astype(jnp.float32)).astype(jnp.bfloat16)
    partial_value = lax.dot_general(
        outage_flow, weighted, (((1,), (1,)), ((), ())), preferred_element_type=jnp.float32
    )
    totals = lax.psum(partial_value, "ctg")
    excess = soft_excess(totals, rating).astype(jnp.bfloat16)
    columns = sens
    return lax.psum_scatter(
        lax.dot_general(
            columns, excess, (((0,), (1,)), ((), ())), preferred_element_type=jnp.float32
        ),
        "line",
        scatter_dimension=0,
        tiled=True,
    )


def solution(mesh):
    in_specs = (
        P(None, ("ctg", "line")),
        P("line", "ctg"),
        P("line", "ctg"),
        P("line"),
        P("line", "ctg"),
        P("ctg", None, None),
        P("ctg"),
    )
    out_specs = P(("ctg", "line"), None)
    return jax.shard_map(
        per_device, mesh=mesh, in_specs=in_specs, out_specs=out_specs, check_vma=False
    )
```

profile of v0, /device:TPU:0, one launch (start us, length us, event | category | flops | bytes accessed | tf_op | source)
XLA Modules:
  0.0 210.2 jit_solution(16124836973732095510)
XLA Ops:
  6.5 0.9 copy.22
  7.4 20.5 %all_to_all.20 = s32[128,1,15]{2,1,0:T(1,128)S(1)} all-to-all(s32[128,1,15]{2,1,0:T(1,128)S(1)} %copy.22), channel_id=1, replica_groups=mesh['ctg'=16,'line'=8] {'ctg','line'}, dimensions={0} | all-to-all | bytes 15360 | tf_op jit(solution)/shard_map/all_to_all | solution.py:14
  27.9 0.1 copy.23
  28.0 0.5 broadcast.84
  28.5 0.8 reduce.5
  29.3 0.2 all_to_all.16
  29.6 0.1 copy.24
  29.7 0.7 copy.25
  30.4 5.0 %gather_fusion = bf16[1920,384]{1,0:T(8,128)(2,1)S(1)} fusion(f32[384,120]{0,1:T(8,128)S(1)} %copy-done.1, s32[2048]{0:T(1024)S(1)} %pad_clamp_fusion), kind=kCustom, calls=%fused_computation | custom fusion | bytes 2956800 | tf_op jit(solution)/shard_map/jit(_take)/gather | solution.py:17
  35.5 0.5 gather.11
  36.0 3.1 %select_convert_fusion = bf16[384,128,15]{0,2,1:T(8,128)(2,1)} fusion(bf16[384,128,15]{0,2,1:T(8,128)(2,1)S(1)} %gather.11, pred[128,15]{1,0:T(8,128)(4,1)} %copy.25, pred[128,15]{1,0:T(8,128)(4,1)S(1)} %copy.24), kind=kLoop, calls=%fused_computation.4 | loop fusion | flops 1474560 | bytes 2952960 | tf_op jit(solution)/shard_map/convert_element_type | solution.py:20
  39.1 4.6 %all-to-all-start.1 = ((bf16[384,128,15]{0,2,1:T(8,128)(2,1)}), bf16[384,128,15]{0,2,1:T(8,128)(2,1)S(1)}, u32[]{:S(2)}, u32[]{:S(2)}) async-start(bf16[384,128,15]{0,2,1:T(8,128)(2,1)} %select_convert_fusion), calls=%async_computation.1 | async-start | bytes 3145728 | tf_op jit(solution)/shard_map/all_to_all | solution.py:19
  43.7 0.0 all-reduce.2.cloned.1.call-start
  43.8 24.8 %all-to-all-done.1 = bf16[384,128,15]{0,2,1:T(8,128)(2,1)S(1)} async-done(((bf16[384,128,15]{0,2,1:T(8,128)(2,1)}), bf16[384,128,15]{0,2,1:T(8,128)(2,1)S(1)}, u32[]{:S(2)}, u32[]{:S(2)}) %all-to-all-start.1) | async-done | bytes 1474592 | tf_op jit(solution)/shard_map/all_to_all | solution.py:19
  68.6 0.5 reshape.60
  69.1 4.1 %gather_fusion.1 = bf16[960,384]{1,0:T(8,128)(2,1)S(1)} fusion(bf16[384,1920]{0,1:T(8,128)(2,1)S(1)} %reshape.60, s32[1024]{0:T(1024)S(1)} %pad_clamp_fusion.1), kind=kCustom, calls=%fused_computation.1 | custom fusion | bytes 1478400 | tf_op jit(solution)/shard_map/jit(_take)/gather | solution.py:27
  73.2 6.7 %fusion = f32[384,1920]{1,0:T(8,128)} fusion(bf16[1920,960]{0,1:T(8,128)(2,1)} %param.8, bf16[1920,960]{0,1:T(8,128)(2,1)} %param.9, bf16[960,384]{1,0:T(8,128)(2,1)S(1)} %gather_fusion.1, pred[960]{0:T(1024)(128)(4,1)S(1)} %compare_and_fusion.1), kind=kOutput, calls=%fused_computation.3 | convolution fusion | flops 1423319040 | bytes 11060160 | tf_op jit(solution)/shard_map/dot_general | solution.py:29
  79.9 0.0 all-reduce.2.cloned.1.call-update
  79.9 0.0 reduce-scatter.4.cloned.1.call-start
  80.0 89.5 %all-reduce.2.cloned.1.call-done = f32[384,1920]{1,0:T(8,128)} async-done(((f32[384,1920]{1,0:T(8,128)}), f32[384,1920]{1,0:T(8,128)}) %all-reduce.2.cloned.1.call-update) | async-done | bytes 2949136 | tf_op jit(solution)/shard_map/psum | solution.py:32
  169.5 3.1 %fusion.2 = f32[128,384]{0,1:T(8,128)S(1)} fusion(bf16[1920,128]{1,0:T(8,128)(2,1)S(1)} %copy-done, f32[384,1920]{1,0:T(8,128)} %all-reduce.2.cloned.1.call-done, f32[1920]{0:T(1024)S(1)} %copy-done.3), kind=kOutput, calls=%fused_computation.7 | convolution fusion | flops 193167360 | bytes 3644928 | tf_op jit(solution)/shard_map/dot_general | solution.py:36
  172.5 0.8 copy.27
  173.3 0.0 reduce-scatter.4.cloned.1.call-update
  173.4 30.0 %reduce-scatter.4.cloned.1.call-done = f32[16,384]{1,0:T(8,128)} async-done(((f32[128,384]{1,0:T(8,128)}), f32[16,384]{1,0:T(8,128)}) %reduce-scatter.4.cloned.1.call-update) | async-done | bytes 24592 | tf_op jit(solution)/shard_map/reduce_scatter | solution.py:35
  (14 shorter events, 0.1 us)
Async XLA Ops:
  6.5 162.9 %copy-start = (bf16[1920,128]{1,0:T(8,128)(2,1)S(1)}, bf16[1920,128]{1,0:T(8,128)(2,1)}, u32[]{:S(2)}) copy-start(bf16[1920,128]{1,0:T(8,128)(2,1)} %param.11) | copy-start | bytes 1474564
  6.5 23.9 %copy-start.1 = (f32[384,120]{0,1:T(8,128)S(1)}, f32[384,120]{0,1:T(8,128)}, u32[]{:S(2)}) copy-start(f32[384,120]{0,1:T(8,128)} %param.7) | copy-start | bytes 552964
  36.0 7.8 %copy-start.2 = (s32[960]{0:T(1024)S(1)}, s32[960]{0:T(1024)}, u32[]{:S(2)}) copy-start(s32[960]{0:T(1024)} %param.13) | copy-start | bytes 11524
  39.1 29.5 %all-to-all-start.1 = ((bf16[384,128,15]{0,2,1:T(8,128)(2,1)}), bf16[384,128,15]{0,2,1:T(8,128)(2,1)S(1)}, u32[]{:S(2)}, u32[]{:S(2)}) async-start(bf16[384,128,15]{0,2,1:T(8,128)(2,1)} %select_convert_fusion), calls=%async_computation.1 | async-start | bytes 3145728 | tf_op jit(solution)/shard_map/all_to_all | solution.py:19
  43.7 125.8 %all-reduce.2.cloned.1.call-start = ((), (), s32[]{:S(2)}) async-start(), calls=%async_computation.3 | async-start | bytes 5898240 | tf_op jit(solution)/shard_map/psum | solution.py:32
  79.9 89.6 %copy-start.3 = (f32[1920]{0:T(1024)S(1)}, f32[1920]{0:T(1024)}, u32[]{:S(2)}) copy-start(f32[1920]{0:T(1024)} %param.10) | copy-start | bytes 23044
  79.9 123.5 %reduce-scatter.4.cloned.1.call-start = ((), (), s32[]{:S(2)}) async-start(), calls=%async_computation.4 | async-start | bytes 221184 | tf_op jit(solution)/shard_map/reduce_scatter | solution.py:35
Sparse Core Ops, SparseCore 0:
  80.1 89.3 all-reduce.1
  173.5 29.8 reduce-scatter.3
where the time goes:
time: 211 us; the launch traced here: 210 us
  waiting for transfers between devices  144 us (68%)
  blocking collectives  20.5 us (10%)
  local copies, waits for them, and re-layouts  13.5 us (6%)
  between operations  13.5 us (6%)
  matrix products  9.77 us (5%)
  starting transfers between devices  4.72 us (2%)
  other arithmetic  3.98 us (2%)
    psum x1, waiting for transfers between devices, per_device(): totals = lax.psum(partial_value, 'ctg')  89.5 us
    reduce_scatter x1, waiting for transfers between devices, per_device(): lax.psum_scatter(lax.dot_general(columns, excess, (((0,), (1,)), ((), ())...  30 us
    all_to_all x1, waiting for transfers between devices, per_device(): lax.all_to_all(jnp.where(live_slot[None], values, 0.0).astype(jnp.bfloat1...  24.8 us
    all_to_all x1, blocking collectives, per_device(): lax.all_to_all(requests, ('ctg', 'line'), split_axis=0, concat_axis=0, ti...  20.5 us
    dot_general x1, matrix products, per_device(): lax.dot_general(outage_flow, weighted, (((1,), (1,)), ((), ())), preferre...  6.72 us
    gather x2, local copies, waits for them, and re-layouts, per_device(): values = jnp.take(base_flow, columns.reshape(-1), axis=1)  5.54 us
    all_to_all x1, starting transfers between devices, per_device(): lax.all_to_all(jnp.where(live_slot[None], values, 0.0).astype(jnp.bfloat1...  4.64 us
  transfers between devices with their start and end apart: 3, of which 3 were waited for; matrix products, arithmetic and copies ran while one was open for 0% of the time, Pallas kernels for 0%

commit v1 on v0

--- a/solution.py
+++ b/solution.py
@@ -29,7 +29,8 @@
     partial_value = lax.dot_general(
         outage_flow, weighted, (((1,), (1,)), ((), ())), preferred_element_type=jnp.float32
     )
-    totals = lax.psum(partial_value, "ctg")
+    shards = lax.all_gather(partial_value, "ctg")
+    totals = jnp.sum(shards, axis=0)
     excess = soft_excess(totals, rating).astype(jnp.bfloat16)
     columns = sens
     return lax.psum_scatter(

time: 211 us -> 400 us (1.90)
  waiting for transfers between devices: 144 us -> 317 us
  other arithmetic: 3.98 us -> 20.4 us
    all_gather x0 -> x1, waiting for transfers between devices: none -> 262 us  [per_device(): shards = lax.all_gather(partial_value, 'ctg')]
    psum x1 -> x0, waiting for transfers between devices: 89.5 us -> none  [per_device(): totals = lax.psum(partial_value, 'ctg')]
    reduce_sum x0 -> x1, other arithmetic: none -> 16.4 us  [per_device(): totals = jnp.sum(shards, axis=0)]
where the time goes in v1:
time: 400 us
  waiting for transfers between devices  317 us (79%)
  blocking collectives  20.5 us (5%)
  other arithmetic  20.4 us (5%)
  local copies, waits for them, and re-layouts  14.4 us (4%)
  between operations  13.5 us (3%)
  matrix products  8.57 us (2%)
  starting transfers between devices  4.72 us (1%)
    all_gather x1, waiting for transfers between devices, per_device(): shards = lax.all_gather(partial_value, 'ctg')  262 us
    reduce_scatter x1, waiting for transfers between devices, per_device(): lax.psum_scatter(lax.dot_general(columns, excess, (((0,), (1,)), ((), ())...  30.5 us
    all_to_all x1, waiting for transfers between devices, per_device(): lax.all_to_all(jnp.where(live_slot[None], values, 0.0).astype(jnp.bfloat1...  24.8 us
    all_to_all x1, blocking collectives, per_device(): lax.all_to_all(requests, ('ctg', 'line'), split_axis=0, concat_axis=0, ti...  20.5 us
    reduce_sum x1, other arithmetic, per_device(): totals = jnp.sum(shards, axis=0)  16.4 us
  transfers between devices with their start and end apart: 3, of which 3 were waited for; matrix products, arithmetic and copies ran while one was open for 0% of the time, Pallas kernels for 0%

profile of v1, /device:TPU:0, one launch (start us, length us, event | category | flops | bytes accessed | tf_op | source)
XLA Modules:
  0.0 399.6 jit_solution(11246675628467044045)
XLA Ops:
  6.5 0.9 copy.22
  7.4 20.5 %all_to_all.20 = s32[128,1,15]{2,1,0:T(1,128)S(1)} all-to-all(s32[128,1,15]{2,1,0:T(1,128)S(1)} %copy.22), channel_id=1, replica_groups=mesh['ctg'=16,'line'=8] {'ctg','line'}, dimensions={0} | all-to-all | bytes 15360 | tf_op jit(solution)/shard_map/all_to_all | solution.py:14
  27.9 0.1 copy.23
  28.0 0.5 broadcast.84
  28.5 0.8 reduce.5
  29.3 0.2 all_to_all.16
  29.6 0.1 copy.24
  29.7 0.7 copy.25
  30.4 5.0 %gather_fusion = bf16[1920,384]{1,0:T(8,128)(2,1)S(1)} fusion(f32[384,120]{0,1:T(8,128)S(1)} %copy-done.1, s32[2048]{0:T(1024)S(1)} %pad_clamp_fusion), kind=kCustom, calls=%fused_computation | custom fusion | bytes 2956800 | tf_op jit(solution)/shard_map/jit(_take)/gather | solution.py:17
  35.5 0.5 gather.11
  36.0 3.1 select_convert_fusion
  39.1 4.6 %all-to-all-start.1 = ((bf16[384,128,15]{0,2,1:T(8,128)(2,1)}), bf16[384,128,15]{0,2,1:T(8,128)(2,1)S(1)}, u32[]{:S(2)}, u32[]{:S(2)}) async-start(bf16[384,128,15]{0,2,1:T(8,128)(2,1)} %select_convert_fusion), calls=%async_computation.1 | async-start | bytes 3145728 | tf_op jit(solution)/shard_map/all_to_all | solution.py:19
  43.7 0.0 all-gather.3.cloned.1.call-start
  43.8 24.8 %all-to-all-done.1 = bf16[384,128,15]{0,2,1:T(8,128)(2,1)S(1)} async-done(((bf16[384,128,15]{0,2,1:T(8,128)(2,1)}), bf16[384,128,15]{0,2,1:T(8,128)(2,1)S(1)}, u32[]{:S(2)}, u32[]{:S(2)}) %all-to-all-start.1) | async-done | bytes 1474592 | tf_op jit(solution)/shard_map/all_to_all | solution.py:19
  68.6 0.5 reshape.60
  69.1 4.1 %gather_fusion.1 = bf16[960,384]{1,0:T(8,128)(2,1)S(1)} fusion(bf16[384,1920]{0,1:T(8,128)(2,1)S(1)} %reshape.60, s32[1024]{0:T(1024)S(1)} %pad_clamp_fusion.1), kind=kCustom, calls=%fused_computation.1 | custom fusion | bytes 1478400 | tf_op jit(solution)/shard_map/jit(_take)/gather | solution.py:27
  73.2 6.7 %fusion = f32[384,1920]{1,0:T(8,128)} fusion(bf16[1920,960]{0,1:T(8,128)(2,1)} %param.8, bf16[1920,960]{0,1:T(8,128)(2,1)} %param.9, bf16[960,384]{1,0:T(8,128)(2,1)S(1)} %gather_fusion.1, pred[960]{0:T(1024)(128)(4,1)S(1)} %compare_and_fusion.1), kind=kOutput, calls=%fused_computation.3 | convolution fusion | flops 1423319040 | bytes 11060160 | tf_op jit(solution)/shard_map/dot_general | solution.py:29
  79.9 0.0 all-gather.3.cloned.1.call-update
  79.9 0.0 reduce-scatter.4.cloned.1.call-start
  80.0 262.2 %all-gather.3.cloned.1.call-done = f32[6144,1920]{1,0:T(8,128)} async-done(((f32[384,1920]{1,0:T(8,128)}), f32[6144,1920]{1,0:T(8,128)}) %all-gather.3.cloned.1.call-update) | async-done | bytes 47185936 | tf_op jit(solution)/shard_map/all_gather | solution.py:32
  342.1 16.4 %reduce_sum.9 = f32[384,1920]{1,0:T(8,128)S(1)} reduce(f32[16,384,1920]{2,1,0:T(8,128)} %bitcast.20, f32[]{:T(128)} %constant.34.clone.1), dimensions={0}, to_apply=%region_0.1 | reduce | flops 11059200 | bytes 50135044 | tf_op jit(solution)/shard_map/reduce_sum | solution.py:33
  358.6 1.9 fusion.2
  360.5 1.7 copy.27
  362.2 30.5 %reduce-scatter.4.cloned.1.call-done = f32[16,384]{1,0:T(8,128)} async-done(((f32[128,384]{1,0:T(8,128)}), f32[16,384]{1,0:T(8,128)}) %reduce-scatter.4.cloned.1.call-update) | async-done | bytes 24592 | tf_op jit(solution)/shard_map/reduce_scatter | solution.py:36
  (15 shorter events, 0.1 us)
Async XLA Ops:
  6.5 352.0 %copy-start = (bf16[1920,128]{1,0:T(8,128)(2,1)S(1)}, bf16[1920,128]{1,0:T(8,128)(2,1)}, u32[]{:S(2)}) copy-start(bf16[1920,128]{1,0:T(8,128)(2,1)} %param.11) | copy-start | bytes 1474564
  6.5 23.9 %copy-start.1 = (f32[384,120]{0,1:T(8,128)S(1)}, f32[384,120]{0,1:T(8,128)}, u32[]{:S(2)}) copy-start(f32[384,120]{0,1:T(8,128)} %param.7) | copy-start | bytes 552964
  36.0 7.8 %copy-start.2 = (s32[960]{0:T(1024)S(1)}, s32[960]{0:T(1024)}, u32[]{:S(2)}) copy-start(s32[960]{0:T(1024)} %param.13) | copy-start | bytes 11524
  39.1 29.5 %all-to-all-start.1 = ((bf16[384,128,15]{0,2,1:T(8,128)(2,1)}), bf16[384,128,15]{0,2,1:T(8,128)(2,1)S(1)}, u32[]{:S(2)}, u32[]{:S(2)}) async-start(bf16[384,128,15]{0,2,1:T(8,128)(2,1)} %select_convert_fusion), calls=%async_computation.1 | async-start | bytes 3145728 | tf_op jit(solution)/shard_map/all_to_all | solution.py:19
  43.7 298.4 %all-gather.3.cloned.1.call-start = ((), (), s32[]{:S(2)}) async-start(), calls=%async_computation.3 | async-start | bytes 50135040 | tf_op jit(solution)/shard_map/all_gather | solution.py:32
  79.9 312.8 %reduce-scatter.4.cloned.1.call-start = ((), (), s32[]{:S(2)}) async-start(), calls=%async_computation.4 | async-start | bytes 221184 | tf_op jit(solution)/shard_map/reduce_scatter | solution.py:36
  342.1 16.4 %copy-start.3 = (f32[1920]{0:T(1024)S(1)}, f32[1920]{0:T(1024)}, u32[]{:S(2)}) copy-start(f32[1920]{0:T(1024)} %param.10) | copy-start | bytes 23044
Sparse Core Ops, SparseCore 0:
  80.0 262.0 all-gather.2
  362.3 30.3 reduce-scatter.3

commit v2 on v0

--- a/solution.py
+++ b/solution.py
@@ -2,6 +2,13 @@
 import jax.numpy as jnp
 from jax import lax
 from jax.sharding import PartitionSpec as P
+
+
+def trade_parts(shard, axis, split, join):
+    size = lax.axis_size(axis)
+    blocks = jnp.stack(jnp.split(shard, size, axis=split), axis=0)
+    blocks = lax.all_to_all(blocks, axis, split_axis=0, concat_axis=0)
+    return jnp.concatenate(blocks, axis=join)
 
 
 def soft_excess(flow_sum, rating):
@@ -16,12 +23,8 @@
     columns = jnp.where(live_slot, asked, 0)
     values = jnp.take(base_flow, columns.reshape(-1), axis=1)
     values = values.reshape(columns_total, asked.shape[0], asked.shape[1])
-    replies = lax.all_to_all(
-        jnp.where(live_slot[None], values, 0.0).astype(jnp.bfloat16),
-        ("ctg", "line"),
-        split_axis=1,
-        concat_axis=1,
-        tiled=True,
+    replies = trade_parts(
+        jnp.where(live_slot[None], values, 0.0).astype(jnp.bfloat16), ("ctg", "line"), 1, 1
     )
     slot_flows = replies.reshape(columns_total, -1)
     outage_flow = jnp.take(slot_flows, ctg_slot, axis=1)

time: 211 us -> 287 us (1.36)
  local copies, waits for them, and re-layouts: 13.5 us -> 90.1 us
    unnamed x9 -> x136, local copies, waits for them, and re-layouts: 0.82 us -> 76.8 us
where the time goes in v2:
time: 287 us; the launch traced here: 286 us
  waiting for transfers between devices  144 us (50%)
  local copies, waits for them, and re-layouts  90.1 us (31%)
  blocking collectives  20.5 us (7%)
  between operations  13.6 us (5%)
  matrix products  9.77 us (3%)
  starting transfers between devices  4.85 us (2%)
  other arithmetic  3.13 us (1%)
    psum x1, waiting for transfers between devices, per_device(): totals = lax.psum(partial_value, 'ctg')  89.5 us
    unnamed x136, local copies, waits for them, and re-layouts  76.8 us
    reduce_scatter x1, waiting for transfers between devices, per_device(): lax.psum_scatter(lax.dot_general(columns, excess, (((0,), (1,)), ((), ())...  30 us
    all_to_all x1, waiting for transfers between devices, trade_parts(): blocks = lax.all_to_all(blocks, axis, split_axis=0, concat_axis=0)  24.8 us
    all_to_all x1, blocking collectives, per_device(): lax.all_to_all(requests, ('ctg', 'line'), split_axis=0, concat_axis=0, ti...  20.5 us
    dot_general x1, matrix products, per_device(): lax.dot_general(outage_flow, weighted, (((1,), (1,)), ((), ())), preferre...  6.72 us
  transfers between devices with their start and end apart: 3, of which 3 were waited for; matrix products, arithmetic and copies ran while one was open for 0% of the time, Pallas kernels for 0%

profile of v2, /device:TPU:0, one launch (start us, length us, event | category | flops | bytes accessed | tf_op | source)
XLA Modules:
  0.0 286.2 jit_solution(13972586393448621400)
XLA Ops:
  6.5 0.9 copy.22
  7.4 20.5 %all_to_all.20 = s32[128,1,15]{2,1,0:T(1,128)S(1)} all-to-all(s32[128,1,15]{2,1,0:T(1,128)S(1)} %copy.22), channel_id=1, replica_groups=mesh['ctg'=16,'line'=8] {'ctg','line'}, dimensions={0} | all-to-all | bytes 15360 | tf_op jit(solution)/shard_map/all_to_all | solution.py:21
  28.5 0.8 reduce.5
  29.7 0.7 copy.25
  30.4 5.0 %gather_fusion = bf16[1920,384]{1,0:T(8,128)(2,1)S(1)} fusion(f32[384,120]{0,1:T(8,128)S(1)} %copy-done.1, s32[2048]{0:T(1024)S(1)} %pad_clamp_fusion), kind=kCustom, calls=%fused_computation | custom fusion | bytes 2956800 | tf_op jit(solution)/shard_map/jit(_take)/gather | solution.py:24
  36.0 2.2 select_convert_fusion
  39.4 0.6 constant_dynamic-update-slice_fusion.125
  49.0 0.6 constant_dynamic-update-slice_fusion.109
  53.8 0.6 constant_dynamic-update-slice_fusion.101
  65.2 0.6 constant_dynamic-update-slice_fusion.82
  82.5 0.6 constant_dynamic-update-slice_fusion.53
  85.5 0.6 constant_dynamic-update-slice_fusion.48
  89.1 0.6 constant_dynamic-update-slice_fusion.42
  90.9 0.6 constant_dynamic-update-slice_fusion.39
  96.9 0.6 constant_dynamic-update-slice_fusion.29
  98.7 0.6 constant_dynamic-update-slice_fusion.26
  114.9 4.8 %all-to-all-start.1 = ((bf16[128,384,1,15]{1,3,2,0:T(8,128)(2,1)}), bf16[128,384,1,15]{1,3,2,0:T(8,128)(2,1)S(1)}, u32[]{:S(2)}, u32[]{:S(2)}) async-start(bf16[128,384,1,15]{1,3,2,0:T(8,128)(2,1)} %constant_dynamic-update-slice_fusion), calls=%async_computation.1 | async-start | bytes 3145728 | tf_op jit(solution)/shard_map/all_to_all | solution.py:10
  119.8 24.8 %all-to-all-done.1 = bf16[128,384,1,15]{1,3,2,0:T(8,128)(2,1)S(1)} async-done(((bf16[128,384,1,15]{1,3,2,0:T(8,128)(2,1)}), bf16[128,384,1,15]{1,3,2,0:T(8,128)(2,1)S(1)}, u32[]{:S(2)}, u32[]{:S(2)}) %all-to-all-start.1) | async-done | bytes 1474592 | tf_op jit(solution)/shard_map/all_to_all | solution.py:10
  145.1 4.1 %gather_fusion.1 = bf16[960,384]{1,0:T(8,128)(2,1)S(1)} fusion(bf16[384,1920]{0,1:T(8,128)(2,1)S(1)} %reshape_reshape.3, s32[1024]{0:T(1024)S(1)} %pad_clamp_fusion.1), kind=kCustom, calls=%fused_computation.1 | custom fusion | bytes 1478400 | tf_op jit(solution)/shard_map/jit(_take)/gather | solution.py:30
  149.2 6.7 %fusion = f32[384,1920]{1,0:T(8,128)} fusion(bf16[1920,960]{0,1:T(8,128)(2,1)} %param.8, bf16[1920,960]{0,1:T(8,128)(2,1)} %param.9, bf16[960,384]{1,0:T(8,128)(2,1)S(1)} %gather_fusion.1, pred[960]{0:T(1024)(128)(4,1)S(1)} %compare_and_fusion.1), kind=kOutput, calls=%fused_computation.3 | convolution fusion | flops 1423319040 | bytes 11060160 | tf_op jit(solution)/shard_map/dot_general | solution.py:32
  156.0 89.5 %all-reduce.2.cloned.1.call-done = f32[384,1920]{1,0:T(8,128)} async-done(((f32[384,1920]{1,0:T(8,128)}), f32[384,1920]{1,0:T(8,128)}) %all-reduce.2.cloned.1.call-update) | async-done | bytes 2949136 | tf_op jit(solution)/shard_map/psum | solution.py:35
  245.5 3.1 %fusion.2 = f32[128,384]{0,1:T(8,128)S(1)} fusion(bf16[1920,128]{1,0:T(8,128)(2,1)S(1)} %copy-done, f32[384,1920]{1,0:T(8,128)} %all-reduce.2.cloned.1.call-done, f32[1920]{0:T(1024)S(1)} %copy-done.3), kind=kOutput, calls=%fused_computation.7 | convolution fusion | flops 193167360 | bytes 3644928 | tf_op jit(solution)/shard_map/dot_general | solution.py:39
  248.5 0.8 copy.27
  249.3 30.0 %reduce-scatter.4.cloned.1.call-done = f32[16,384]{1,0:T(8,128)} async-done(((f32[128,384]{1,0:T(8,128)}), f32[16,384]{1,0:T(8,128)}) %reduce-scatter.4.cloned.1.call-update) | async-done | bytes 24592 | tf_op jit(solution)/shard_map/reduce_scatter | solution.py:38
  (142 shorter events, 72.7 us)
Async XLA Ops:
  6.5 238.9 %copy-start = (bf16[1920,128]{1,0:T(8,128)(2,1)S(1)}, bf16[1920,128]{1,0:T(8,128)(2,1)}, u32[]{:S(2)}) copy-start(bf16[1920,128]{1,0:T(8,128)(2,1)} %param.11) | copy-start | bytes 1474564
  6.5 23.9 %copy-start.1 = (f32[384,120]{0,1:T(8,128)S(1)}, f32[384,120]{0,1:T(8,128)}, u32[]{:S(2)}) copy-start(f32[384,120]{0,1:T(8,128)} %param.7) | copy-start | bytes 552964
  114.9 4.8 %copy-start.2 = (s32[960]{0:T(1024)S(1)}, s32[960]{0:T(1024)}, u32[]{:S(2)}) copy-start(s32[960]{0:T(1024)} %param.13) | copy-start | bytes 11524
  114.9 29.6 %all-to-all-start.1 = ((bf16[128,384,1,15]{1,3,2,0:T(8,128)(2,1)}), bf16[128,384,1,15]{1,3,2,0:T(8,128)(2,1)S(1)}, u32[]{:S(2)}, u32[]{:S(2)}) async-start(bf16[128,384,1,15]{1,3,2,0:T(8,128)(2,1)} %constant_dynamic-update-slice_fusion), calls=%async_computation.1 | async-start | bytes 3145728 | tf_op jit(solution)/shard_map/all_to_all | solution.py:10
  119.7 125.8 %all-reduce.2.cloned.1.call-start = ((), (), s32[]{:S(2)}) async-start(), calls=%async_computation.3 | async-start | bytes 5898240 | tf_op jit(solution)/shard_map/psum | solution.py:35
  155.9 89.6 %copy-start.3 = (f32[1920]{0:T(1024)S(1)}, f32[1920]{0:T(1024)}, u32[]{:S(2)}) copy-start(f32[1920]{0:T(1024)} %param.10) | copy-start | bytes 23044
  155.9 123.5 %reduce-scatter.4.cloned.1.call-start = ((), (), s32[]{:S(2)}) async-start(), calls=%async_computation.4 | async-start | bytes 221184 | tf_op jit(solution)/shard_map/reduce_scatter | solution.py:38
Sparse Core Ops, SparseCore 0:
  156.0 89.3 all-reduce.1
  249.5 29.8 reduce-scatter.3
